TPU v7x, 32 devices: a whole 2x2x4 slice. The times are simulated.
32 devices in a mesh: dp: 2 (over core), cent: 16 (over z, y, x).
Axes of the slice: x: 2, y: 2, z: 4, core: 2. Of those that a mesh axis runs over, the one named last changes fastest.
Arguments:
- embeddings: bfloat16 [16384, 1024], P(('dp', 'cent')), may hold values from -44.5 to 53.875
- centroids: float32 [8192, 1024], P(('dp', 'cent')), may hold values from -3 to 5
- candidates: int32 [64, 8], P(('dp', 'cent')), may hold values from 0 to 15, all different within a row; in each aligned block of 32 rows (0 to 31, 32 to 63, ...) at most 24 rows name the same one
Outputs:
- new_centroids: float32 [8192, 1024], P(('dp', 'cent'))
- log_norm: float32 [16384], P(('dp', 'cent'))
- objective: float32 [], replicated
Inputs may be any that keep to these rules, and one draw needn't show every extreme that they name: `candidates`: the 8 entries of a row block are different. Among the row blocks of one coarse group (aligned runs of 32 row blocks), no centroid block is named more than 24 times, and some centroid block is named exactly 24 times in every draw.
All inputs are finite; a program needn't handle non-finite values.
Results may differ from a plain program's by a relative error of at most 0.0067.
Values may be sent and summed in bfloat16 or wider, within the bound.
A program may use at most 128 MiB of HBM per device.

v0:
```python
import math

import jax
import jax.numpy as jnp
from jax import lax
from jax.sharding import PartitionSpec as P

BLK = 256
TOPC = 8


floor_value = -1e30


def merged(value, axis, join):
    pieces = jax.tree.map(lambda part: lax.all_gather(part, axis), value)
    head = jax.tree.map(lambda part: part[0], pieces)
    tail = jax.tree.map(lambda part: part[1:], pieces)
    running, _ = lax.scan(lambda running, share: (join(running, share), None), head, tail)
    return running


def combine_stats(left_pair, right_pair):
    peak_value = jnp.maximum(left_pair[0], right_pair[0])
    total_value = left_pair[1] * jnp.exp(left_pair[0] - peak_value) + right_pair[1] * jnp.exp(
        right_pair[0] - peak_value
    )
    return (peak_value, total_value)


def per_device(embeddings, centroids, candidates):
    cent_count = lax.axis_size("cent")
    own_index = lax.axis_index("cent")
    block_len = BLK
    feature_dim = embeddings.shape[1]
    own_row_blocks = candidates.shape[0]
    own_blocks = centroids.shape[0] // block_len
    group_blocks = own_row_blocks * cent_count
    slot_count = min(own_row_blocks * cent_count, 3 * own_row_blocks * TOPC // (2 * own_blocks))
    cent_blocks = centroids.astype(jnp.bfloat16).reshape(own_blocks, block_len, feature_dim)
    half_norm = 0.5 * jnp.sum(centroids * centroids, axis=1).reshape(own_blocks, block_len)
    group_rows, group_lists = (
        lax.all_gather(embeddings, "cent", axis=0, tiled=True),
        lax.all_gather(candidates, "cent", axis=0, tiled=True),
    )
    grouped = group_rows.reshape(group_blocks, block_len, feature_dim)
    own_ids = own_index * own_blocks + jnp.arange(own_blocks, dtype=jnp.int32)
    requested = jnp.any(group_lists[:, :, None] == own_ids[None, None, :], axis=1)
    block_iota = jnp.arange(group_blocks, dtype=jnp.int32)
    sort_keys = jnp.where(requested, 0, group_blocks) + block_iota[:, None]
    slot_blocks = jnp.argsort(sort_keys, axis=0)[:slot_count]
    slot_live = jnp.take_along_axis(requested, slot_blocks, axis=0)
    picked = grouped[slot_blocks]
    dot_scores = jnp.einsum(
        "mjbd,jkd->mjbk", picked, cent_blocks, preferred_element_type=jnp.float32
    )
    live_mask = slot_live[:, :, None, None]
    logits = (dot_scores - half_norm[None, :, None, :]) / math.sqrt(feature_dim)
    logits = jnp.where(live_mask, logits, floor_value)
    local_peak = jnp.max(logits, axis=3)
    local_total = jnp.where(
        slot_live[:, :, None], jnp.sum(jnp.exp(logits - local_peak[..., None]), axis=3), 0.0
    )
    peak_rows = (
        jnp.full((group_blocks, block_len), floor_value, jnp.float32)
        .at[slot_blocks]
        .max(local_peak)
    )
    scaled_total = local_total * jnp.exp(local_peak - peak_rows[slot_blocks])
    total_rows = jnp.zeros((group_blocks, block_len), jnp.float32).at[slot_blocks].add(scaled_total)
    global_peak, global_total = merged((peak_rows, total_rows), "cent", combine_stats)
    log_group = global_peak + jnp.log(global_total)
    log_norm = lax.dynamic_slice_in_dim(
        log_group, own_index * own_row_blocks, own_row_blocks, 0
    ).reshape(-1)
    weights = jnp.where(live_mask, jnp.exp(logits - log_group[slot_blocks][..., None]), 0.0)
    counts = jnp.sum(weights, axis=(0, 2))
    weights_bf = weights.astype(jnp.bfloat16)
    block_sums = jnp.einsum(
        "mjbk,mjbd->jkd", weights_bf, picked, preferred_element_type=jnp.float32
    )
    old_blocks = centroids.reshape(own_blocks, block_len, feature_dim)
    new_blocks = (block_sums + old_blocks) / (counts[..., None] + 1.0)
    new_centroids = new_blocks.reshape(own_blocks * block_len, feature_dim)
    row_total_count = embeddings.shape[0] * lax.axis_size("dp") * cent_count
    objective = lax.psum(jnp.sum(log_norm), ("dp", "cent")) / row_total_count
    return (new_centroids, log_norm, objective)


def solution(mesh):
    in_specs = (P(("dp", "cent"), None), P(("dp", "cent"), None), P(("dp", "cent"), None))
    out_specs = (P(("dp", "cent"), None), P(("dp", "cent")), P())
    return jax.shard_map(
        per_device, mesh=mesh, in_specs=in_specs, out_specs=out_specs, check_vma=False
    )
```

profile of v0, /device:TPU:0, one launch (start us, length us, event | category | flops | bytes accessed | tf_op | source)
XLA Modules:
  0.0 372.1 jit_solution(4079944136693221693)
XLA Ops:
  7.2 0.0 all-gather.5.cloned.1.call-start
  7.2 0.7 all-gather.5.cloned.1.call-update
  7.9 43.1 %all-gather.2 = s32[16,2,8]{2,1,0:T(2,128)S(1)} all-gather(s32[1,2,8]{2,1,0:T(2,128)} %bitcast.106), channel_id=1, replica_groups=mesh['dp'=2,'cent'=16] {'cent'}, dimensions={0}, use_global_device_ids=true | all-gather | bytes 1088 | tf_op jit(solution)/shard_map/all_gather | solution.py:44
  51.0 0.4 compare_reduce_fusion
  51.3 0.1 reshape.219
  51.5 0.1 copy.10
  51.6 0.8 sort.17
  52.4 0.1 fusion.37
  52.5 0.7 gather_fusion
  53.2 0.1 copy.11
  53.3 0.1 select_reduce_fusion
  53.4 1.7 multiply_reduce_fusion
  55.1 150.1 %all-gather.5.cloned.1.call-done = bf16[8192,1024]{1,0:T(8,128)(2,1)} async-done(((bf16[512,1024]{1,0:T(8,128)(2,1)}), bf16[8192,1024]{1,0:T(8,128)(2,1)}) %all-gather.5.cloned.1.call-update) | async-done | bytes 16777232 | tf_op jit(solution)/shard_map/all_gather | solution.py:43
  205.2 0.0 copy-start.2
  205.2 12.0 %gather_fusion.1 = bf16[24,256,1024]{2,1,0:T(8,128)(2,1)} fusion(bf16[32,256,1024]{2,1,0:T(8,128)(2,1)} %bitcast.101, s32[1024]{0:T(1024)S(1)} %pad_clamp_fusion), kind=kCustom, calls=%fused_computation.1 | custom fusion | bytes 25165920 | tf_op jit(solution)/shard_map/gather | solution.py:53
  217.2 0.0 copy-done.2
  217.2 6.6 %fusion.13 = (f32[24,256]{1,0:T(8,128)S(1)}, f32[24,256,256]{1,2,0:T(8,128)S(1)}) fusion(f32[256]{0:T(256)S(1)} %broadcast_multiply_fusion, pred[24]{0:T(512)(128)(4,1)S(1)} %select_reduce_fusion, bf16[24,256,1024]{2,1,0:T(8,128)(2,1)} %gather_fusion.1, f32[256,1024]{1,0:T(8,128)S(1)} %copy-done.2), kind=kOutput, calls=%fused_computation.23 | convolution fusion | flops 3227772928 | bytes 19948568 | tf_op jit(solution)/shard_map/mjbd,jkd->mjbk/dot_general | solution.py:54
  223.8 0.0 copy-start
  223.8 2.7 copy-done
  226.5 1.8 exponential_reduce_fusion
  228.3 0.7 scatter_custom_fusion
  229.1 0.8 scatter_custom_fusion.1
  229.9 41.3 %all-gather.1 = f32[512,256]{1,0:T(8,128)S(1)} all-gather(f32[32,256]{1,0:T(8,128)S(1)} %scatter_custom_fusion.1), channel_id=3, replica_groups=mesh['dp'=2,'cent'=16] {'cent'}, dimensions={0}, use_global_device_ids=true | all-gather | bytes 557056 | tf_op jit(solution)/shard_map/all_gather | solution.py:16
  271.3 38.3 %all-gather = f32[512,256]{1,0:T(8,128)S(1)} all-gather(f32[32,256]{1,0:T(8,128)S(1)} %scatter_custom_fusion), channel_id=2, replica_groups=mesh['dp'=2,'cent'=16] {'cent'}, dimensions={0}, use_global_device_ids=true | all-gather | bytes 557056 | tf_op jit(solution)/shard_map/all_gather | solution.py:16
  309.6 0.8 while.12
  310.4 0.6 gather_fusion.2
  311.0 0.0 copy-start.1
  311.0 4.5 %fusion.5 = f32[256]{0:T(256)S(1)} fusion(f32[24,256]{1,0:T(8,128)S(1)} %gather_fusion.2, f32[256]{0:T(256)S(1)} %broadcast_multiply_fusion, f32[24,256,256]{1,2,0:T(8,128)} %copy-done, pred[24]{0:T(512)(128)(4,1)S(1)} %select_reduce_fusion), kind=kLoop, calls=%fused_computation.17 | loop fusion | flops 9436928 | bytes 6318104 | tf_op jit(solution)/shard_map/reduce_sum | solution.py:77
  315.6 0.1 copy-done.1
  315.7 9.3 %fusion.22 = f32[256,1024]{1,0:T(8,128)} fusion(f32[256,1024]{1,0:T(8,128)S(1)} %copy-done.2, bf16[24,256,1024]{2,1,0:T(8,128)(2,1)} %gather_fusion.1, f32[24,256]{1,0:T(8,128)S(1)} %gather_fusion.2, f32[256]{0:T(256)S(1)} %broadcast_multiply_fusion, f32[24,256,256]{1,2,0:T(8,128)S(1)} %copy-done.1, pred[24]{0:T(512)(128)(4,1)S(1)} %select_reduce_fusion, ...), kind=kOutput, calls=%fused_computation.28 | convolution fusion | flops 3231186944 | bytes 20998168 | tf_op jit(solution)/shard_map/mjbk,mjbd->jkd/dot_general | solution.py:79
  325.0 0.6 dynamic-slice_reduce_fusion
  325.6 0.6 copy.12
  326.2 37.3 %psum.7 = f32[]{:T(128)} all-reduce(f32[]{:T(128)} %get-tuple-element.47), channel_id=1, replica_groups=mesh['dp'=2,'cent'=16] {'dp','cent'}, use_global_device_ids=true, to_apply=%region_11.12 | all-reduce | flops 1 | bytes 8 | tf_op jit(solution)/shard_map/psum | solution.py:86
  (26 shorter events, 0.6 us)
Async XLA Ops:
  7.2 198.1 %all-gather.5.cloned.1.call-start = ((), (), s32[]{:S(2)}) async-start(), calls=%async_computation | async-start | bytes 17825792 | tf_op jit(solution)/shard_map/all_gather | solution.py:43
  205.2 12.0 %copy-start.2 = (f32[256,1024]{1,0:T(8,128)S(1)}, f32[256,1024]{1,0:T(8,128)}, u32[]{:S(2)}) copy-start(f32[256,1024]{1,0:T(8,128)} %param.6) | copy-start | bytes 3145732
  223.8 2.7 copy-start
  311.0 4.6 %copy-start.1 = (f32[24,256,256]{1,2,0:T(8,128)S(1)}, f32[24,256,256]{1,2,0:T(8,128)}, u32[]{:S(2)}) copy-start(f32[24,256,256]{1,2,0:T(8,128)} %copy-done) | copy-start | bytes 18874372
Sparse Core Ops, SparseCore 0:
  10.8 194.4 all-gather.4
where the time goes:
time: 374 us; the launch traced here: 372 us
  blocking collectives  160 us (43%)
  waiting for transfers between devices  151 us (40%)
  local copies, waits for them, and re-layouts  17 us (5%)
  matrix products  15.9 us (4%)
  between operations  15.9 us (4%)
  other arithmetic  12.1 us (3%)
    all_gather x1, waiting for transfers between devices, per_device(): lax.all_gather(embeddings, 'cent', axis=0, tiled=True)  150 us
    all_gather x2, blocking collectives, merged(): pieces = jax.tree.map(lambda part: lax.all_gather(part, axis), value)  79.6 us
    all_gather x1, blocking collectives, per_device(): lax.all_gather(candidates, 'cent', axis=0, tiled=True)  43.1 us
    psum x1, blocking collectives, per_device(): objective = lax.psum(jnp.sum(log_norm), ('dp', 'cent')) / row_total_count  37.3 us
    gather x1, local copies, waits for them, and re-layouts, per_device(): picked = grouped[slot_blocks]  12 us
    dot_general x1, matrix products, per_device(): jnp.einsum('mjbk,mjbd->jkd', weights_bf, picked, preferred_element_type=j...  9.31 us
  transfers between devices with their start and end apart: 1, of which 1 were waited for; matrix products, arithmetic and copies ran while one was open for 1% of the time, Pallas kernels for 0%

commit v1 on v0

v1 whole, which is shorter than its diff:
```python
import functools
import math

import jax
import jax.numpy as jnp
from jax import lax
from jax.experimental import pallas as pl
from jax.experimental.pallas import tpu as pltpu
from jax.sharding import PartitionSpec as P

BLK = 256
PLANE = 4
FLOOR = -1e30
MESH = pl.DeviceIdType.MESH


def kernel(
    nd, nz, row_total,
    emb_ref, cent_ref, mask_ref,
    new_ref, log_ref, obj_ref,
    rbuf, cbuf, hnrow, hncol, maskbuf, pbuf, mst, sst, stat, fbuf, wbuf, part, tx, up_rx, dn_rx,
    cacc, cnt, cnt_rx, zsum, gsum,
    local_sem, row_s, row_r, mask_s, mask_r, hn_s, hn_r, cu_s, cu_r, cd_s, cd_r,
    st_s, st_r, zs_s, zs_r, gs_s, gs_r, ct_s, ct_r, up_s, up_r, dn_s, dn_r,
):
    d = lax.axis_index("dp")
    me = lax.axis_index("cent")
    p, q = me // PLANE, me % PLANE
    x, y = q % 2, q // 2
    qx, qy, qd = q + 1 - 2 * x, q + 2 - 4 * y, 3 - q
    last = nz - 1
    blk, dim = cent_ref.shape

    def at_plane(o):
        return {"cent": p * PLANE + o}

    def at_z(z):
        return {"cent": z * PLANE + q}

    def rows_at(o, b):
        return rbuf.at[pl.ds(pl.multiple_of((o * 2 + b) * BLK, BLK), BLK)]

    def remote(src, dst, s, r, to):
        return pltpu.make_async_remote_copy(
            src_ref=src, dst_ref=dst, send_sem=s, recv_sem=r, device_id=to, device_id_type=MESH
        )

    own_rows = pl.ds(pl.multiple_of(q * 2 * BLK, 2 * BLK), 2 * BLK)
    fetch = pltpu.make_async_copy(emb_ref, rbuf.at[own_rows], local_sem)
    fetch.start()

    barrier = pltpu.get_barrier_semaphore()
    for o in (qx, qy, qd):
        pl.semaphore_signal(barrier, inc=1, device_id=at_plane(o), device_id_type=MESH)
    for k in range(1, nz):
        pl.semaphore_signal(barrier, inc=1, device_id=at_z((p + k) % nz), device_id_type=MESH)
    for k in range(1, nd):
        pl.semaphore_signal(barrier, inc=1, device_id={"dp": (d + k) % nd}, device_id_type=MESH)

    cent = cent_ref[...]
    cbuf[p] = cent.astype(jnp.bfloat16)
    norm = 0.5 * jnp.sum(cent * cent, axis=1, keepdims=True)
    wide = jnp.broadcast_to(norm, (blk, 128))
    hncol[p] = wide
    hnrow[p] = wide.T[:8]
    maskbuf[pl.ds(q * 2, 2)] = mask_ref[...]
    fetch.wait()
    pl.semaphore_wait(barrier, 3 + (nz - 1) + (nd - 1))

    plane_peers = (qx, qy, qd)
    mine = maskbuf.at[pl.ds(q * 2, 2)]
    mask_out = [remote(mine, mine, mask_s.at[i], mask_r.at[i], at_plane(o)) for i, o in enumerate(plane_peers)]
    hn_out = [
        remote(hnrow.at[p], hnrow.at[p], hn_s.at[k - 1], hn_r.at[k - 1], at_z((p + k) % nz)) for k in range(1, nz)
    ]
    for c in mask_out + hn_out:
        c.start()

    def up_send(s):
        z = jnp.maximum(p - s, 0)
        return remote(cbuf.at[z], cbuf.at[z], cu_s.at[s], cu_r.at[s], at_z(jnp.minimum(p + 1, last)))

    def dn_send(s):
        z = jnp.minimum(p + s, last)
        return remote(cbuf.at[z], cbuf.at[z], cd_s.at[s], cd_r.at[s], at_z(jnp.maximum(p - 1, 0)))

    def up_wait(s):
        z = p - 1 - s
        remote(cbuf.at[z], cbuf.at[z], cu_s.at[s], cu_r.at[s], at_z(p - 1)).wait_recv()

    def dn_wait(s):
        z = p + 1 + s
        remote(cbuf.at[z], cbuf.at[z], cd_s.at[s], cd_r.at[s], at_z(p + 1)).wait_recv()

    def row_copy(i, o, b, to):
        return remote(rows_at(o, b), rows_at(o, b), row_s.at[i], row_r.at[i], at_plane(to))

    pl.when(p < last)(lambda: up_send(0).start())
    pl.when(p > 0)(lambda: dn_send(0).start())
    row_out = [
        row_copy(0, q, 0, qx),
        row_copy(1, q, 1, qy),
        row_copy(2, q, 1, qx),
        row_copy(3, q, 0, qy),
        row_copy(4, qx, 0, qy),
        row_copy(5, qy, 1, qx),
    ]
    for c in row_out[:4]:
        c.start()
    row_in = [
        row_copy(0, qx, 0, qx),
        row_copy(1, qy, 1, qy),
        row_copy(2, qx, 1, qx),
        row_copy(3, qy, 0, qy),
        row_copy(4, qd, 0, qy),
        row_copy(5, qd, 1, qx),
    ]

    for i, o in enumerate(plane_peers):
        there = maskbuf.at[pl.ds(o * 2, 2)]
        remote(there, there, mask_s.at[i], mask_r.at[i], at_plane(o)).wait_recv()
    for k in range(1, nz):
        z = (p + nz - k) % nz
        remote(hnrow.at[z], hnrow.at[z], hn_s.at[k - 1], hn_r.at[k - 1], at_z(z)).wait_recv()
        row = hnrow[z][:1]
        hncol[z] = jnp.broadcast_to(row, (128, blk)).T

    def pair(i, z):
        t, e = i // 2, i % 2
        mult = (t * (3 - t)) // 2
        late = mult * (t - 1)
        rel = t - late + mult * e
        b = e + late * (1 - 2 * e)
        rx, ry = rel % 2, rel // 2
        ox, oy = x + rx - 2 * x * rx, y + ry - 2 * y * ry
        ci = (oy * 2 + ox) * 2 + b
        start = pl.multiple_of(ci * BLK, BLK)
        dots = lax.dot_general(
            cbuf[z], rbuf[pl.ds(start, BLK), :], (((1,), (1,)), ((), ())), preferred_element_type=jnp.float32
        )
        bias = maskbuf[ci, pl.ds(z * PLANE + q, 1), :]
        bias = jnp.concatenate([bias] * (BLK // 128), axis=1)
        norm = jnp.concatenate([hncol[z]] * (BLK // 128), axis=1)
        logits = (dots - norm) * (1.0 / math.sqrt(dim)) + bias
        peak = jnp.max(logits, axis=0, keepdims=True)
        e_val = jnp.exp(logits - peak)
        pbuf[z, :, pl.ds(start, BLK)] = e_val
        mst[z, pl.ds(ci, 1), :] = peak
        sst[z, pl.ds(ci, 1), :] = jnp.sum(e_val, axis=0, keepdims=True)

    def pairs(row_lo, row_hi, z_lo, z_hi):
        count = row_hi - row_lo

        def body(n, carry):
            pair(row_lo + n % count, z_lo + n // count)
            return carry

        lax.fori_loop(0, count * (z_hi - z_lo), body, 0)

    pairs(0, 2, p, p + 1)
    for s in range(last):
        @pl.when(p - 1 - s >= 0)
        def _(s=s):
            up_wait(s)
            if s + 1 < last:
                pl.when(p < last)(lambda: up_send(s + 1).start())

        @pl.when(p + 1 + s <= last)
        def _(s=s):
            dn_wait(s)
            if s + 1 < last:
                pl.when(p > 0)(lambda: dn_send(s + 1).start())

        row_in[2 * s].wait_recv()
        row_in[2 * s + 1].wait_recv()
        if s == 0:
            row_out[4].start()
            row_out[5].start()
        have = 2 * s + 2

        @pl.when(p - 1 - s >= 0)
        def _(s=s, have=have):
            pairs(0, have, p - 1 - s, p - s)

        @pl.when(p + 1 + s <= last)
        def _(s=s, have=have):
            pairs(0, have, p + 1 + s, p + 2 + s)

        pairs(have, have + 2, jnp.maximum(p - s - 1, 0), jnp.minimum(p + s + 1, last) + 1)

    peak, total = mst[0], sst[0]
    for z in range(1, nz):
        peak = jnp.maximum(peak, mst[z])
    total = sum(sst[z] * jnp.exp(mst[z] - peak) for z in range(nz))
    stat[q, 0] = peak
    stat[q, 1] = total
    st_out = [
        remote(stat.at[q], stat.at[q], st_s.at[i], st_r.at[i], at_plane(o)) for i, o in enumerate(plane_peers)
    ]
    for c in st_out:
        c.start()
    for i, o in enumerate(plane_peers):
        remote(stat.at[o], stat.at[o], st_s.at[i], st_r.at[i], at_plane(o)).wait_recv()
    peak = stat[0, 0]
    for o in range(1, PLANE):
        peak = jnp.maximum(peak, stat[o, 0])
    total = sum(stat[o, 1] * jnp.exp(stat[o, 0] - peak) for o in range(PLANE))
    log_norm = peak + jnp.log(total)
    place = lax.broadcasted_iota(jnp.int32, log_norm.shape, 0)
    for r in range(2):
        log_ref[r : r + 1, :] = jnp.sum(jnp.where(place == q * 2 + r, log_norm, 0.0), axis=0, keepdims=True)
    for z in range(nz):
        fbuf[z] = jnp.exp(mst[z] - log_norm)
    zsum[p] = jnp.broadcast_to(jnp.sum(jnp.sum(log_norm, axis=1, keepdims=True), axis=0, keepdims=True), (8, 128))
    zs_out = [
        remote(zsum.at[p], zsum.at[p], zs_s.at[k - 1], zs_r.at[k - 1], at_z((p + k) % nz)) for k in range(1, nz)
    ]
    for c in zs_out:
        c.start()

    def partial(t):
        cacc[...] = jnp.zeros_like(cacc)

        def weigh(ci, carry):
            cols = pl.ds(pl.multiple_of(ci * BLK, BLK), BLK)
            w = pbuf[t, :, cols] * fbuf[t, pl.ds(ci, 1), :]
            wbuf[:, cols] = w.astype(jnp.bfloat16)
            acc = cacc[...]
            for j in range(BLK // 128):
                acc = acc + w[:, j * 128 : (j + 1) * 128]
            cacc[...] = acc
            return carry

        lax.fori_loop(0, 2 * PLANE, weigh, 0)
        col = jnp.broadcast_to(jnp.sum(cacc[...], axis=1, keepdims=True), (blk, 128))
        cnt[t] = col.T[:8]

        def tile(n, carry):
            cols = pl.ds(pl.multiple_of(n * BLK, BLK), BLK)
            part[t, :, cols] = jnp.dot(wbuf[...], rbuf[:, cols], preferred_element_type=jnp.float32)
            return carry

        lax.fori_loop(0, dim // BLK, tile, 0)

    def up_copy(t):
        return remote(tx.at[t], up_rx.at[t], up_s.at[t], up_r.at[t], at_z(jnp.minimum(p + 1, last)))

    def dn_copy(t):
        return remote(tx.at[t], dn_rx.at[t], dn_s.at[t], dn_r.at[t], at_z(jnp.maximum(p - 1, 0)))

    for s in range(last):
        up_t, dn_t = last - s, s

        @pl.when(p < up_t)
        def _(t=up_t):
            partial(t)

            @pl.when(p == 0)
            def _():
                tx[t] = part[t].astype(jnp.bfloat16)
                up_copy(t).start()

        @pl.when(p > dn_t)
        def _(t=dn_t):
            partial(t)

            @pl.when(p == last)
            def _():
                tx[t] = part[t].astype(jnp.bfloat16)
                dn_copy(t).start()

    partial(p)

    cnt_rx[p] = cnt[p]
    ct_out = [
        remote(cnt.at[(p + k) % nz], cnt_rx.at[p], ct_s.at[k - 1], ct_r.at[k - 1], at_z((p + k) % nz))
        for k in range(1, nz)
    ]
    for c in ct_out:
        c.start()

    for k in range(1, nz):
        z = (p + nz - k) % nz
        remote(zsum.at[z], zsum.at[z], zs_s.at[k - 1], zs_r.at[k - 1], at_z(z)).wait_recv()
    gsum[d] = sum(zsum[z] for z in range(nz))
    gs_out = [
        remote(gsum.at[d], gsum.at[d], gs_s.at[k - 1], gs_r.at[k - 1], {"dp": (d + k) % nd}) for k in range(1, nd)
    ]
    for c in gs_out:
        c.start()

    for s in range(last):
        up_t, dn_t = last - s, s

        @pl.when((p > 0) & (p < up_t))
        def _(t=up_t):
            up_copy(t).wait_recv()
            tx[t] = (part[t] + up_rx[t].astype(jnp.float32)).astype(jnp.bfloat16)
            up_copy(t).start()

        @pl.when((p < last) & (p > dn_t))
        def _(t=dn_t):
            dn_copy(t).wait_recv()
            tx[t] = (part[t] + dn_rx[t].astype(jnp.float32)).astype(jnp.bfloat16)
            dn_copy(t).start()

    for k in range(1, nz):
        z = (p + nz - k) % nz
        remote(cnt.at[z], cnt_rx.at[z], ct_s.at[k - 1], ct_r.at[k - 1], at_z(z)).wait_recv()
    counts = sum(cnt_rx[z] for z in range(nz))
    scale = 1.0 / (jnp.broadcast_to(counts[:1], (128, blk)).T[:, :1] + 1.0)
    for k in range(1, nd):
        o = (d + nd - k) % nd
        remote(gsum.at[o], gsum.at[o], gs_s.at[k - 1], gs_r.at[k - 1], {"dp": o}).wait_recv()
    obj_ref[...] = sum(gsum[o] for o in range(nd)) / row_total

    new_ref[...] = cent_ref[...] + part[p]

    @pl.when(p > 0)
    def _():
        up_copy(p).wait_recv()
        new_ref[...] += up_rx[p].astype(jnp.float32)

    @pl.when(p < last)
    def _():
        dn_copy(p).wait_recv()
        new_ref[...] += dn_rx[p].astype(jnp.float32)

    new_ref[...] = new_ref[...] * scale

    for c in mask_out + hn_out + row_out + st_out + zs_out + ct_out + gs_out:
        c.wait_send()
    for s in range(last):
        pl.when((p < last) & (p - s >= 0))(lambda s=s: up_send(s).wait_send())
        pl.when((p > 0) & (p + s <= last))(lambda s=s: dn_send(s).wait_send())
        pl.when(p < last - s)(lambda s=s: up_copy(last - s).wait_send())
        pl.when(p > s)(lambda s=s: dn_copy(s).wait_send())


def per_device(embeddings, centroids, candidates):
    nd, nc = lax.axis_size("dp"), lax.axis_size("cent")
    nz = nc // PLANE
    dim = embeddings.shape[1]
    rows = embeddings.shape[0]
    rb = candidates.shape[0]
    named = jnp.any(candidates[:, :, None] == jnp.arange(nc, dtype=jnp.int32), axis=1)
    mask = jnp.broadcast_to(jnp.where(named, 0.0, FLOOR).astype(jnp.float32)[:, :, None], (rb, nc, 128))
    f32, bf16 = jnp.float32, jnp.bfloat16
    nrb = rb * PLANE
    dma = pltpu.SemaphoreType.DMA
    vmem = pl.BlockSpec(memory_space=pltpu.VMEM)
    new, logs, obj = pl.pallas_call(
        functools.partial(kernel, nd, nz, float(rows * nd * nc)),
        out_shape=(
            jax.ShapeDtypeStruct((BLK, dim), f32),
            jax.ShapeDtypeStruct((rb, BLK), f32),
            jax.ShapeDtypeStruct((8, 128), f32),
        ),
        in_specs=[pl.BlockSpec(memory_space=pl.ANY), vmem, vmem],
        out_specs=(vmem, vmem, vmem),
        scratch_shapes=[
            pltpu.VMEM((nrb * BLK, dim), bf16),
            pltpu.VMEM((nz, BLK, dim), bf16),
            pltpu.VMEM((nz, 8, BLK), f32),
            pltpu.VMEM((nz, BLK, 128), f32),
            pltpu.VMEM((nrb, nc, 128), f32),
            pltpu.VMEM((nz, BLK, nrb * BLK), f32),
            pltpu.VMEM((nz, nrb, BLK), f32),
            pltpu.VMEM((nz, nrb, BLK), f32),
            pltpu.VMEM((PLANE, 2, nrb, BLK), f32),
            pltpu.VMEM((nz, nrb, BLK), f32),
            pltpu.VMEM((BLK, nrb * BLK), bf16),
            pltpu.VMEM((nz, BLK, dim), f32),
            pltpu.VMEM((nz, BLK, dim), bf16),
            pltpu.VMEM((nz, BLK, dim), bf16),
            pltpu.VMEM((nz, BLK, dim), bf16),
            pltpu.VMEM((BLK, 128), f32),
            pltpu.VMEM((nz, 8, BLK), f32),
            pltpu.VMEM((nz, 8, BLK), f32),
            pltpu.VMEM((nz, 8, 128), f32),
            pltpu.VMEM((nd, 8, 128), f32),
            dma(()),
            dma((6,)), dma((6,)),
            dma((3,)), dma((3,)),
            dma((nz - 1,)), dma((nz - 1,)),
            dma((nz - 1,)), dma((nz - 1,)),
            dma((nz - 1,)), dma((nz - 1,)),
            dma((3,)), dma((3,)),
            dma((nz - 1,)), dma((nz - 1,)),
            dma((max(nd - 1, 1),)), dma((max(nd - 1, 1),)),
            dma((nz - 1,)), dma((nz - 1,)),
            dma((nz,)), dma((nz,)),
            dma((nz,)), dma((nz,)),
        ],
        compiler_params=pltpu.CompilerParams(
            collective_id=0, has_side_effects=True, vmem_limit_bytes=48 * 1024 * 1024
        ),
    )(embeddings, centroids, mask)
    return new, logs.reshape(rows), obj[0, 0]


def solution(mesh):
    in_specs = (P(("dp", "cent"), None), P(("dp", "cent"), None), P(("dp", "cent"), None))
    out_specs = (P(("dp", "cent"), None), P(("dp", "cent")), P())
    return jax.shard_map(
        per_device, mesh=mesh, in_specs=in_specs, out_specs=out_specs, check_vma=False
    )
```

time: 374 us -> 104 us (0.28)
  blocking collectives: 160 us -> 0 us
  waiting for transfers between devices: 151 us -> 0 us
  Pallas kernels: 0 us -> 97.6 us
  matrix products: 15.9 us -> 0 us
  between operations: 15.9 us -> 0.64 us
  local copies, waits for them, and re-layouts: 17 us -> 4.58 us
  other arithmetic: 12.1 us -> 0.78 us
    all_gather x1 -> x0, waiting for transfers between devices: 150 us -> none  [per_device(): lax.all_gather(embeddings, 'cent', axis=0, tiled=True)]
    all_gather x3 -> x0, blocking collectives: 123 us -> none  [the longest x2 79.6 us: merged(): pieces = jax.tree.map(lambda part: lax.all_gather(part, axis), value)]
    pallas_call x0 -> x1, Pallas kernels: none -> 97.6 us  [per_device(): pl.pallas_call(functools.partial(kernel, nd, nz, float(rows * nd * nc)),...]
    psum x1 -> x0, blocking collectives: 37.3 us -> none  [per_device(): objective = lax.psum(jnp.sum(log_norm), ('dp', 'cent')) / row_total_count]
    dot_general x2 -> x0, matrix products: 15.9 us -> none  [the longest x1 9.31 us: per_device(): jnp.einsum('mjbk,mjbd->jkd', weights_bf, picked, preferred_element_type=j...]
    gather x4 -> x0, local copies, waits for them, and re-layouts: 13.4 us -> none  [the longest x1 12 us: per_device(): picked = grouped[slot_blocks]]
    reduce_sum x4 -> x0, other arithmetic: 8.64 us -> none  [the longest x1 4.52 us: per_device(): counts = jnp.sum(weights, axis=(0, 2))]
  transfers between devices with their start and end apart: 1 -> 0, of which waited for: 1 -> 0; matrix products, arithmetic and copies ran while one was open for 1% -> 0% of each run, Pallas kernels for 0% -> 0%
where the time goes in v1:
time: 104 us
  Pallas kernels  97.6 us (94%)
  local copies, waits for them, and re-layouts  4.58 us (4%)
    pallas_call x1, Pallas kernels, per_device(): pl.pallas_call(functools.partial(kernel, nd, nz, float(rows * nd * nc)),...  97.6 us
    unnamed x6, local copies, waits for them, and re-layouts  4 us

profile of v1, /device:TPU:0, one launch (start us, length us, event | category | flops | bytes accessed | tf_op | source)
XLA Modules:
  0.0 103.6 jit_solution(393752560053970002)
XLA Ops:
  0.6 0.8 fusion
  1.4 0.1 broadcast_in_dim.18.mask_ref
  1.5 0.0 copy-start
  1.5 1.2 %copy-done = bf16[512,1024]{1,0:T(8,128)(2,1)S(1)} copy-done((bf16[512,1024]{1,0:T(8,128)(2,1)S(1)}, bf16[512,1024]{1,0:T(8,128)(2,1)}, u32[]{:S(2)}) %copy-start) | copy-done | bytes 1048600
  2.7 0.0 copy-start.1
  2.7 1.2 %copy-done.1 = f32[256,1024]{1,0:T(8,128)S(1)} copy-done((f32[256,1024]{1,0:T(8,128)S(1)}, f32[256,1024]{1,0:T(8,128)}, u32[]{:S(2)}) %copy-start.1) | copy-done | bytes 1048600
  3.9 97.6 %shard_map.58 = (f32[256,1024]{1,0:T(8,128)S(1)}, f32[2,256]{1,0:T(2,128)S(1)}, f32[8,128]{1,0:T(8,128)S(1)}) custom-call(bf16[512,1024]{1,0:T(8,128)(2,1)S(1)} %copy-done, f32[256,1024]{1,0:T(8,128)S(1)} %copy-done.1, f32[2,16,128]{2,1,0:T(8,128)S(1)} %broadcast_in_dim.18.mask_ref), custom_call_target="tpu_custom_call" | custom-call | tf_op jit(solution)/shard_map/pallas_call | solution.py:352
  101.6 0.5 slice.3
  102.1 0.6 copy.6
  102.6 1.0 copy.8
  (1 shorter events, 0.0 us)
Async XLA Ops:
  1.5 1.2 %copy-start = (bf16[512,1024]{1,0:T(8,128)(2,1)S(1)}, bf16[512,1024]{1,0:T(8,128)(2,1)}, u32[]{:S(2)}) copy-start(bf16[512,1024]{1,0:T(8,128)(2,1)} %emb_ref.1) | copy-start | bytes 3145732
  2.7 1.2 %copy-start.1 = (f32[256,1024]{1,0:T(8,128)S(1)}, f32[256,1024]{1,0:T(8,128)}, u32[]{:S(2)}) copy-start(f32[256,1024]{1,0:T(8,128)} %cent_ref.1) | copy-start | bytes 3145732

commit v2 on v1

--- a/solution.py
+++ b/solution.py
@@ -10,6 +10,7 @@
 
 BLK = 256
 PLANE = 4
+HALVES = 2
 FLOOR = -1e30
 MESH = pl.DeviceIdType.MESH
 
@@ -30,6 +31,7 @@
     qx, qy, qd = q + 1 - 2 * x, q + 2 - 4 * y, 3 - q
     last = nz - 1
     blk, dim = cent_ref.shape
+    half = blk // HALVES
 
     def at_plane(o):
         return {"cent": p * PLANE + o}
@@ -149,10 +151,12 @@
         sst[z, pl.ds(ci, 1), :] = jnp.sum(e_val, axis=0, keepdims=True)
 
     def pairs(row_lo, row_hi, z_lo, z_hi):
-        count = row_hi - row_lo
+        count = (row_hi - row_lo) // 2
 
         def body(n, carry):
-            pair(row_lo + n % count, z_lo + n // count)
+            i, z = row_lo + 2 * (n % count), z_lo + n // count
+            pair(i, z)
+            pair(i + 1, z)
             return carry
 
         lax.fori_loop(0, count * (z_hi - z_lo), body, 0)
@@ -242,11 +246,18 @@
 
         lax.fori_loop(0, dim // BLK, tile, 0)
 
-    def up_copy(t):
-        return remote(tx.at[t], up_rx.at[t], up_s.at[t], up_r.at[t], at_z(jnp.minimum(p + 1, last)))
-
-    def dn_copy(t):
-        return remote(tx.at[t], dn_rx.at[t], dn_s.at[t], dn_r.at[t], at_z(jnp.maximum(p - 1, 0)))
+    def up_copy(t, h):
+        part_of = (t, pl.ds(h * half, half))
+        return remote(
+            tx.at[part_of], up_rx.at[part_of], up_s.at[t, h], up_r.at[t, h], at_z(jnp.minimum(p + 1, last))
+        )
+
+    def dn_copy(t, h):
+        part_of = (t, pl.ds(h * half, half))
+        return remote(tx.at[part_of], dn_rx.at[part_of], dn_s.at[t, h], dn_r.at[t, h], at_z(jnp.maximum(p - 1, 0)))
+
+    up_order = [(last - s, h) for s in range(last) for h in range(HALVES)]
+    dn_order = [(s, h) for s in range(last) for h in range(HALVES)]
 
     for s in range(last):
         up_t, dn_t = last - s, s
@@ -258,7 +269,9 @@
             @pl.when(p == 0)
             def _():
                 tx[t] = part[t].astype(jnp.bfloat16)
-                up_copy(t).start()
+                if t == last:
+                    for n in range(2):
+                        up_copy(*up_order[n]).start()
 
         @pl.when(p > dn_t)
         def _(t=dn_t):
@@ -267,7 +280,9 @@
             @pl.when(p == last)
             def _():
                 tx[t] = part[t].astype(jnp.bfloat16)
-                dn_copy(t).start()
+                if t == 0:
+                    for n in range(2):
+                        dn_copy(*dn_order[n]).start()
 
     partial(p)
 
@@ -289,20 +304,33 @@
     for c in gs_out:
         c.start()
 
-    for s in range(last):
-        up_t, dn_t = last - s, s
+    for n in range(len(up_order)):
+        up_t, dn_t = up_order[n][0], dn_order[n][0]
 
         @pl.when((p > 0) & (p < up_t))
-        def _(t=up_t):
-            up_copy(t).wait_recv()
-            tx[t] = (part[t] + up_rx[t].astype(jnp.float32)).astype(jnp.bfloat16)
-            up_copy(t).start()
+        def _(t=up_t, h=up_order[n][1]):
+            up_copy(t, h).wait_recv()
+            rows = pl.ds(h * half, half)
+            tx[t, rows] = (part[t, rows] + up_rx[t, rows].astype(jnp.float32)).astype(jnp.bfloat16)
+            up_copy(t, h).start()
 
         @pl.when((p < last) & (p > dn_t))
-        def _(t=dn_t):
-            dn_copy(t).wait_recv()
-            tx[t] = (part[t] + dn_rx[t].astype(jnp.float32)).astype(jnp.bfloat16)
-            dn_copy(t).start()
+        def _(t=dn_t, h=dn_order[n][1]):
+            dn_copy(t, h).wait_recv()
+            rows = pl.ds(h * half, half)
+            tx[t, rows] = (part[t, rows] + dn_rx[t, rows].astype(jnp.float32)).astype(jnp.bfloat16)
+            dn_copy(t, h).start()
+
+        if n >= 2:
+            @pl.when(p == 0)
+            def _(n=n):
+                up_copy(*up_order[n - 2]).wait_send()
+                up_copy(*up_order[n]).start()
+
+            @pl.when(p == last)
+            def _(n=n):
+                dn_copy(*dn_order[n - 2]).wait_send()
+                dn_copy(*dn_order[n]).start()
 
     for k in range(1, nz):
         z = (p + nz - k) % nz
@@ -315,16 +343,18 @@
     obj_ref[...] = sum(gsum[o] for o in range(nd)) / row_total
 
     new_ref[...] = cent_ref[...] + part[p]
-
-    @pl.when(p > 0)
-    def _():
-        up_copy(p).wait_recv()
-        new_ref[...] += up_rx[p].astype(jnp.float32)
-
-    @pl.when(p < last)
-    def _():
-        dn_copy(p).wait_recv()
-        new_ref[...] += dn_rx[p].astype(jnp.float32)
+    for h in range(HALVES):
+        rows = pl.ds(h * half, half)
+
+        @pl.when(p > 0)
+        def _(h=h, rows=rows):
+            up_copy(p, h).wait_recv()
+            new_ref[rows, :] += up_rx[p, rows].astype(jnp.float32)
+
+        @pl.when(p < last)
+        def _(h=h, rows=rows):
+            dn_copy(p, h).wait_recv()
+            new_ref[rows, :] += dn_rx[p, rows].astype(jnp.float32)
 
     new_ref[...] = new_ref[...] * scale
 
@@ -333,8 +363,11 @@
     for s in range(last):
         pl.when((p < last) & (p - s >= 0))(lambda s=s: up_send(s).wait_send())
         pl.when((p > 0) & (p + s <= last))(lambda s=s: dn_send(s).wait_send())
-        pl.when(p < last - s)(lambda s=s: up_copy(last - s).wait_send())
-        pl.when(p > s)(lambda s=s: dn_copy(s).wait_send())
+    tail = len(up_order) - 2
+    for n in range(len(up_order)):
+        up_t, dn_t = up_order[n][0], dn_order[n][0]
+        pl.when((p < up_t) & ((p > 0) | (n >= tail)))(lambda n=n: up_copy(*up_order[n]).wait_send())
+        pl.when((p > dn_t) & ((p < last) | (n >= tail)))(lambda n=n: dn_copy(*dn_order[n]).wait_send())
 
 
 def per_device(embeddings, centroids, candidates):
@@ -389,8 +422,8 @@
             dma((nz - 1,)), dma((nz - 1,)),
             dma((max(nd - 1, 1),)), dma((max(nd - 1, 1),)),
             dma((nz - 1,)), dma((nz - 1,)),
-            dma((nz,)), dma((nz,)),
-            dma((nz,)), dma((nz,)),
+            dma((nz, HALVES)), dma((nz, HALVES)),
+            dma((nz, HALVES)), dma((nz, HALVES)),
         ],
         compiler_params=pltpu.CompilerParams(
             collective_id=0, has_side_effects=True, vmem_limit_bytes=48 * 1024 * 1024

time: 104 us -> 96.6 us (0.929)
  Pallas kernels: 97.6 us -> 90 us
    pallas_call x1, Pallas kernels: 97.6 us -> 90 us  [per_device(): pl.pallas_call(functools.partial(kernel, nd, nz, float(rows * nd * nc)),...]
where the time goes in v2:
time: 96.6 us; the launch traced here: 96 us
  Pallas kernels  90 us (93%)
  local copies, waits for them, and re-layouts  4.58 us (5%)
    pallas_call x1, Pallas kernels, per_device(): pl.pallas_call(functools.partial(kernel, nd, nz, float(rows * nd * nc)),...  90 us
    unnamed x6, local copies, waits for them, and re-layouts  4 us

profile of v2, /device:TPU:0, one launch (start us, length us, event | category | flops | bytes accessed | tf_op | source)
XLA Modules:
  0.0 96.0 jit_solution(11768652560936504844)
XLA Ops:
  0.6 0.8 fusion
  1.4 0.1 broadcast_in_dim.18.mask_ref
  1.5 0.0 copy-start
  1.5 1.2 %copy-done = bf16[512,1024]{1,0:T(8,128)(2,1)S(1)} copy-done((bf16[512,1024]{1,0:T(8,128)(2,1)S(1)}, bf16[512,1024]{1,0:T(8,128)(2,1)}, u32[]{:S(2)}) %copy-start) | copy-done | bytes 1048600
  2.7 0.0 copy-start.1
  2.7 1.2 %copy-done.1 = f32[256,1024]{1,0:T(8,128)S(1)} copy-done((f32[256,1024]{1,0:T(8,128)S(1)}, f32[256,1024]{1,0:T(8,128)}, u32[]{:S(2)}) %copy-start.1) | copy-done | bytes 1048600
  3.9 90.0 %shard_map.58 = (f32[256,1024]{1,0:T(8,128)S(1)}, f32[2,256]{1,0:T(2,128)S(1)}, f32[8,128]{1,0:T(8,128)S(1)}) custom-call(bf16[512,1024]{1,0:T(8,128)(2,1)S(1)} %copy-done, f32[256,1024]{1,0:T(8,128)S(1)} %copy-done.1, f32[2,16,128]{2,1,0:T(8,128)S(1)} %broadcast_in_dim.18.mask_ref), custom_call_target="tpu_custom_call" | custom-call | tf_op jit(solution)/shard_map/pallas_call | solution.py:385
  94.0 0.5 slice.3
  94.5 0.6 copy.6
  95.1 1.0 %copy.8 = f32[256,1024]{1,0:T(8,128)} copy(f32[256,1024]{1,0:T(8,128)S(1)} %get-tuple-element.12) | data formatting | bytes 2097152
  (1 shorter events, 0.0 us)
Async XLA Ops:
  1.5 1.2 %copy-start = (bf16[512,1024]{1,0:T(8,128)(2,1)S(1)}, bf16[512,1024]{1,0:T(8,128)(2,1)}, u32[]{:S(2)}) copy-start(bf16[512,1024]{1,0:T(8,128)(2,1)} %emb_ref.1) | copy-start | bytes 3145732
  2.7 1.2 %copy-start.1 = (f32[256,1024]{1,0:T(8,128)S(1)}, f32[256,1024]{1,0:T(8,128)}, u32[]{:S(2)}) copy-start(f32[256,1024]{1,0:T(8,128)} %cent_ref.1) | copy-start | bytes 3145732
